TPU v7x, 512 devices: a whole 4x4x16 slice. The times are simulated.
512 devices in a mesh: rep: 32 (over z, y_hi), fsdp: 16 (over x, y_lo, core).
Axes of the slice: x: 4, y: 4 (y_hi: 2, y_lo: 2; y = y_hi * 2 + y_lo), z: 16, core: 2. Of those that a mesh axis runs over, the one named last changes fastest.
Arguments:
- tokens: bfloat16 [114688, 8192], P(('rep', 'fsdp')), may hold values from -24 to 24
- cotangent: bfloat16 [114688, 256], P(('rep', 'fsdp')), may hold values from -6 to 6
- weight: float32 [32, 8192, 256], P('rep', 'fsdp'), may hold values from -6 to 6
- gain: float32 [32, 8192], P('rep', 'fsdp'), may hold values from 0.5 to 1.5
- step: int32 [], replicated, may hold values from 0 to 999
Outputs:
- keys_values: bfloat16 [114688, 256], P(('rep', 'fsdp'))
- new_weight: float32 [32, 8192, 256], P('rep', 'fsdp')
- new_gain: float32 [32, 8192], P('rep', 'fsdp')
All inputs are finite; a program needn't handle non-finite values.
Results may differ from a plain program's by a relative error of at most 0.0065.
Values may be sent and summed in bfloat16 or wider, within the bound.
A program may use at most 64 MiB of HBM per device.

v0:
```python
import jax
import jax.numpy as jnp
from jax import lax
from jax.sharding import PartitionSpec as P

learn_rate = 0.25
gain_rate = 0.01


def from_behind(block, axis, distance):
    devices = range(lax.axis_size(axis))
    route = [((i - distance) % len(devices), i) for i in devices]
    return lax.ppermute(block, axis, route)


def late_mover(bit):
    return lambda block: from_behind(block, "rep", 1 << bit)


def body(tokens, cotangent, weight, gain, step):
    width = tokens.shape[1]
    scale = width ** (-0.5)
    levels = lax.axis_size("rep").bit_length() - 1
    master, gains = weight[0], gain[0]
    rows, columns = master.shape
    which = step % levels

    w_half = master.astype(jnp.bfloat16).astype(jnp.float32)
    g_half = gains.astype(jnp.bfloat16).astype(jnp.float32)
    whole_w = lax.all_gather(
        (w_half * g_half[:, None]).astype(jnp.bfloat16), "fsdp", axis=0, tiled=True
    )
    values = tokens.astype(jnp.float32)
    inverse = lax.rsqrt(jnp.mean(values * values, -1, keepdims=True) + 1e-05) * scale
    scaled = (cotangent.astype(jnp.float32) * inverse).astype(jnp.bfloat16)
    part = lax.dot_general(
        tokens, scaled, (((0,), (0,)), ((), ())), preferred_element_type=jnp.float32
    ).astype(jnp.bfloat16)
    product = lax.psum_scatter(part, "fsdp", scatter_dimension=0, tiled=True).astype(jnp.float32)
    keys_values = (
        jnp.dot(tokens, whole_w, preferred_element_type=jnp.float32) * inverse
    ).astype(jnp.bfloat16)
    upd_weight = master - learn_rate * (g_half[:, None] * product)
    upd_gain = gains - gain_rate * jnp.sum(w_half * product, 1)
    gain_rows = rows // columns
    payload = jnp.concatenate(
        [upd_weight, upd_gain.reshape(gain_rows, columns), jnp.zeros((16 - gain_rows, columns))], 0
    ).astype(jnp.bfloat16)
    other = lax.switch(which, [late_mover(bit) for bit in range(levels)], payload)
    other = other.astype(jnp.float32)
    new_weight = 0.5 * (upd_weight + other[:rows])
    new_gain = 0.5 * (upd_gain + other[rows : rows + gain_rows].reshape(rows))
    return (keys_values, new_weight[None], new_gain[None])


def solution(mesh):
    return jax.shard_map(
        body,
        mesh=mesh,
        in_specs=(
            P(("rep", "fsdp"), None),
            P(("rep", "fsdp"), None),
            P("rep", "fsdp", None),
            P("rep", "fsdp"),
            P(),
        ),
        out_specs=(P(("rep", "fsdp"), None), P("rep", "fsdp", None), P("rep", "fsdp")),
        check_vma=False,
    )
```

profile of v0, /device:TPU:1, one launch (start us, length us, event | category | flops | bytes accessed | tf_op | source)
XLA Modules:
  0.0 165.3 jit_solution(14720819113076986586)
XLA Ops:
  7.2 0.0 reduce-scatter.2.cloned.1.call-start
  7.2 3.0 %multiply_reduce_fusion = f32[224]{0:T(256)S(1)} fusion(bf16[224,8192]{1,0:T(8,128)(2,1)} %param.10), kind=kLoop, calls=%fused_computation.2 | loop fusion | flops 5504800 | bytes 3670912 | tf_op jit(solution)/shard_map/reduce_sum | solution.py:34
  10.2 0.1 copy-done
  10.4 4.3 %fusion = bf16[8192,256]{0,1:T(8,128)(2,1)} fusion(bf16[224,8192]{1,0:T(8,128)(2,1)S(1)} %copy-done, bf16[224,256]{1,0:T(8,128)(2,1)} %param.11, f32[224]{0:T(256)S(1)} %rsqrt_multiply_fusion), kind=kOutput, calls=%fused_computation.1 | convolution fusion | flops 941793280 | bytes 7979904 | tf_op jit(solution)/shard_map/dot_general | solution.py:36
  14.6 0.0 all-gather.2.cloned.1.call-start
  15.4 0.2 copy.27
  15.6 0.5 broadcast.37
  16.1 0.7 fusion.11
  16.8 0.1 pad.2.clone
  16.8 75.5 %reduce-scatter.2.cloned.1.call-done = bf16[512,256]{0,1:T(8,128)(2,1)} async-done(((bf16[8192,256]{0,1:T(8,128)(2,1)}), bf16[512,256]{0,1:T(8,128)(2,1)}) %reduce-scatter.2.cloned.1.call-update) | async-done | bytes 262160 | tf_op jit(solution)/shard_map/reduce_scatter | solution.py:39
  92.4 1.2 fusion.9
  93.6 0.1 copy.28
  93.7 0.1 maximum_maximum_fusion
  93.8 9.5 %conditional.1 = (bf16[528,256]{1,0:T(8,128)(2,1)}) conditional(s32[]{:T(128)} %clamp.3, bf16[528,256]{0,1:T(8,128)(2,1)S(1)} %maximum_maximum_fusion, bf16[528,256]{0,1:T(8,128)(2,1)S(1)} %maximum_maximum_fusion, bf16[528,256]{0,1:T(8,128)(2,1)S(1)} %maximum_maximum_fusion, ...), branch_computations={%region_3.4_spmd, %region_4.5_spmd, %region_5.6_spmd, %region_6.7_... | conditional | bytes 1622064 | solution.py:49
  93.8 0.1 copy.30
  94.0 2.8 %collective-permute-start.1 = (bf16[528,256]{1,0:T(8,128)(2,1)S(1)}, bf16[528,256]{1,0:T(8,128)(2,1)}, u32[]{:S(2)}, u32[]{:S(2)}) collective-permute-start(bf16[528,256]{1,0:T(8,128)(2,1)S(1)} %copy.30), channel_id=1, source_target_pairs={{480,0},{496,16},{0,32},{16,48},{32,64},{48,80},{64,96},{80,112},{... | collective-permute-start | bytes 811016 | tf_op jit(solution)/shard_map/cond/branch_1_fun/ppermute | solution.py:13
  96.7 6.5 %collective-permute-done.1 = bf16[528,256]{1,0:T(8,128)(2,1)} collective-permute-done((bf16[528,256]{1,0:T(8,128)(2,1)S(1)}, bf16[528,256]{1,0:T(8,128)(2,1)}, u32[]{:S(2)}, u32[]{:S(2)}) %collective-permute-start.1) | collective-permute-done | bytes 270368 | tf_op jit(solution)/shard_map/cond/branch_1_fun/ppermute | solution.py:13
  103.3 1.2 copy.34
  104.5 0.9 fusion.8
  105.4 0.1 copy.35
  105.5 1.0 copy.36
  106.5 0.6 add_multiply_fusion
  107.1 46.1 %all-gather.2.cloned.1.call-done = bf16[8192,256]{0,1:T(8,128)(2,1)} async-done(((bf16[512,256]{0,1:T(8,128)(2,1)}), bf16[8192,256]{0,1:T(8,128)(2,1)}) %all-gather.2.cloned.1.call-update) | async-done | bytes 4194320 | tf_op jit(solution)/shard_map/all_gather | solution.py:30
  153.1 5.4 %fusion.2 = bf16[224,256]{1,0:T(8,128)(2,1)} fusion(bf16[8192,256]{0,1:T(8,128)(2,1)} %all-gather.2.cloned.1.call-done, bf16[224,8192]{1,0:T(8,128)(2,1)} %param.10, f32[224]{0:T(256)S(1)} %rsqrt_multiply_fusion), kind=kOutput, calls=%fused_computation.5 | convolution fusion | flops 939638784 | bytes 7979904 | tf_op jit(solution)/shard_map/dot_general | solution.py:41
  (18 shorter events, 0.2 us)
Async XLA Ops:
  7.2 85.2 %reduce-scatter.2.cloned.1.call-start = ((), (), s32[]{:S(2)}) async-start(), calls=%async_computation.2 | async-start | bytes 4456448 | tf_op jit(solution)/shard_map/reduce_scatter | solution.py:39
  7.2 3.1 %copy-start = (bf16[224,8192]{1,0:T(8,128)(2,1)S(1)}, bf16[224,8192]{1,0:T(8,128)(2,1)}, u32[]{:S(2)}) copy-start(bf16[224,8192]{1,0:T(8,128)(2,1)} %param.10) | copy-start | bytes 11010052
  10.4 5.0 %copy-start.2 = (f32[1,512,256]{2,1,0:T(8,128)S(1)}, f32[1,512,256]{2,1,0:T(8,128)}, u32[]{:S(2)}) copy-start(f32[1,512,256]{2,1,0:T(8,128)} %param.12) | copy-start | bytes 1572868
  14.6 1.5 copy-start.3
  14.6 138.5 %all-gather.2.cloned.1.call-start = ((), (), s32[]{:S(2)}) async-start(), calls=%async_computation.1 | async-start | bytes 4456448 | tf_op jit(solution)/shard_map/all_gather | solution.py:30
  92.4 12.1 %copy-start.1 = (bf16[512,256]{0,1:T(8,128)(2,1)S(1)}, bf16[512,256]{0,1:T(8,128)(2,1)}, u32[]{:S(2)}) copy-start(bf16[512,256]{0,1:T(8,128)(2,1)} %reduce-scatter.2.cloned.1.call-done) | copy-start | bytes 786436
  94.0 9.3 %collective-permute-start.1 = (bf16[528,256]{1,0:T(8,128)(2,1)S(1)}, bf16[528,256]{1,0:T(8,128)(2,1)}, u32[]{:S(2)}, u32[]{:S(2)}) collective-permute-start(bf16[528,256]{1,0:T(8,128)(2,1)S(1)} %copy.30), channel_id=1, source_target_pairs={{480,0},{496,16},{0,32},{16,48},{32,64},{48,80},{64,96},{80,112},{... | collective-permute-start | bytes 811016 | tf_op jit(solution)/shard_map/cond/branch_1_fun/ppermute | solution.py:13
Sparse Core Ops, SparseCore 0:
  14.8 77.5 reduce-scatter.1
  105.5 47.5 all-gather.1
where the time goes:
time: 166 us; the launch traced here: 165 us
  waiting for transfers between devices  128 us (77%)
  between operations  14.8 us (9%)
  matrix products  9.62 us (6%)
  other arithmetic  6.4 us (4%)
  local copies, waits for them, and re-layouts  3.5 us (2%)
  starting transfers between devices  2.83 us (2%)
    reduce_scatter x1, waiting for transfers between devices, body(): lax.psum_scatter(part, 'fsdp', scatter_dimension=0, tiled=True)  75.5 us
    all_gather x1, waiting for transfers between devices, body(): lax.all_gather((w_half * g_half[:, None]).astype(jnp.bfloat16), 'fsdp', a...  46.1 us
    ppermute x1, waiting for transfers between devices, from_behind(): return lax.ppermute(block, axis, route)  6.53 us
    dot_general x1, matrix products, body(): jnp.dot(tokens, whole_w, preferred_element_type=jnp.float32) * inverse  5.36 us
    dot_general x1, matrix products, body(): lax.dot_general(tokens, scaled, (((0,), (0,)), ((), ())), preferred_eleme...  4.26 us
  transfers between devices with their start and end apart: 3, of which 3 were waited for; matrix products, arithmetic and copies ran while one was open for 2% of the time, Pallas kernels for 0%

commit v1 on v0

v1 whole, which is shorter than its diff:
```python
import functools

import jax
import jax.numpy as jnp
from jax import lax
from jax.experimental import pallas as pl
from jax.experimental.pallas import tpu as pltpu
from jax.sharding import PartitionSpec as P

learn_rate = 0.25
gain_rate = 0.01
MESH = pl.DeviceIdType.MESH
F32, BF16 = jnp.float32, jnp.bfloat16
N_SUB = 2
MESSAGES = 96


def kernel(
    distance, n_rep, tokens, cotangent, weight, gain, kv_out, weight_out, gain_out,
    tok, tok_rest, cot, master, gains, gain_cols, scaled, inverse, part_a, part_b, whole_w,
    from_a1, from_a2, from_a3, from_b1, from_b2, from_b3, payload, other, upd, upd_gain,
    total, from_sibling, local_sem, send_sem, recv_sem,
):
    rep, fsdp = lax.axis_index("rep"), lax.axis_index("fsdp")
    n_fsdp = lax.axis_size("fsdp")
    x, y, core = fsdp // 4, (fsdp // 2) % 2, fsdp % 2
    mate = 1 - y
    sibling = (rep, fsdp + 1 - 2 * core)
    across = (rep, fsdp + 2 - 4 * y)
    right = (rep, (fsdp + 4) % n_fsdp)
    left = (rep, (fsdp + n_fsdp - 4) % n_fsdp)
    ahead = ((rep + distance) % n_rep, fsdp)
    behind = ((rep + n_rep - distance) % n_rep, fsdp)
    at = [(x + j) % 4 for j in range(4)]
    rows_y = (y, mate)
    n_tok = cotangent.shape[0]
    width = tokens.shape[1]
    shard, kv = master.shape
    sub = shard // N_SUB
    half = sub // 2
    scale = width**-0.5

    barrier = pltpu.get_barrier_semaphore()
    for partner in (sibling, across, right, left, ahead, behind):
        pl.semaphore_signal(barrier, inc=1, device_id=partner, device_id_type=MESH)

    def load(source, target, index):
        copy = pltpu.make_async_copy(source, target, local_sem.at[index])
        copy.start()
        return copy

    load_w = load(weight.at[0], master, 0)
    load_g = load(gain, gains, 1)
    load_c = load(cotangent, cot, 2)
    load_t = []
    for block in range(8):
        for mine in (True, False):
            column = 1024 * block + 512 * (core if mine else 1 - core)
            source = tokens.at[:, pl.ds(pl.multiple_of(column, 512), 512)]
            target = tok.at[block // 2, block % 2, pl.ds(0, n_tok)] if mine else tok_rest.at[block]
            load_t.append((load(source, target, 3 + len(load_t)), target))

    names = {}
    sent = []

    def message(name, source, target, device):
        index = names.setdefault(name, len(names))
        assert index < MESSAGES
        return pltpu.make_async_remote_copy(
            src_ref=source, dst_ref=target, send_sem=send_sem.at[index],
            recv_sem=recv_sem.at[index], device_id=device, device_id_type=MESH,
        )

    def send(name, source, target, device):
        copy = message(name, source, target, device)
        copy.start()
        sent.append(copy)

    def receive(name, target, device):
        message(name, target, target, device).wait_recv()

    load_w.wait()
    load_g.wait()
    gb_row = gains[...].astype(BF16).astype(F32)
    for k in range(shard // 128):
        block = slice(128 * k, 128 * k + 128)
        column = jnp.broadcast_to(gb_row[:, block], (128, 128)).T
        gain_cols[block] = column
        wb = master[block].astype(BF16).astype(F32)
        whole_w[x, y, k // 2, k % 2] = (wb * jnp.concatenate([column, column], 1)).astype(BF16)

    pl.semaphore_wait(barrier, 6)

    for name, device in (("g1y", across), ("g1r", right), ("g1l", left)):
        send(name, whole_w.at[x, y], whole_w.at[x, y], device)
    order = [(j, q) for j in (2, 1, 3, 0) for q in (1, 0)]
    theirs = pl.ds(n_tok, n_tok)
    for s in range(N_SUB):
        for j, q in order:
            column = 512 * (4 * at[j] + 2 * rows_y[q] + 1 - core) + sub * s
            send(
                f"t{s}{j}{q}", tokens.at[:, pl.ds(pl.multiple_of(column, sub), sub)],
                tok.at[at[j], rows_y[q], theirs, pl.ds(sub * s, sub)], sibling,
            )

    squares = jnp.zeros((n_tok, 128), F32)
    for copy, target in load_t:
        copy.wait()
        for k in range(4):
            value = target[:, 128 * k : 128 * k + 128].astype(F32)
            squares = squares + value * value
    inverse_now = lax.rsqrt(jnp.sum(squares, 1, keepdims=True) * (1.0 / width) + 1e-05) * scale
    inverse[...] = jnp.broadcast_to(inverse_now, (n_tok, 128))
    load_c.wait()
    scaled[0:n_tok] = (cot[...].astype(F32) * inverse_now).astype(BF16)
    send("cot", scaled.at[pl.ds(0, n_tok)], scaled.at[theirs], sibling)
    receive("cot", scaled.at[theirs], sibling)

    for s in range(N_SUB):
        columns = pl.ds(sub * s, sub)
        for j, q in order:
            target = tok.at[at[j], rows_y[q], theirs, columns]
            receive(f"t{s}{j}{q}", target, sibling)
            product = lax.dot_general(
                tok[at[j], rows_y[q], :, columns], scaled[...], (((0,), (0,)), ((), ())),
                preferred_element_type=F32,
            ).astype(BF16)
            part_a[at[j], s, rows_y[q]] = product[:half].reshape(2, half // 2, kv)
            part_b[at[j], s, rows_y[q]] = product[half:].reshape(2, half // 2, kv)
            if q == 1:
                send(f"b1{s}{j}", part_b.at[at[j], s, mate], from_b1.at[s, j], across)
            elif j == 2:
                send(f"a1r{s}", part_a.at[at[2], s, :, 0], from_a1.at[s, 0], right)
                send(f"a1l{s}", part_a.at[at[2], s, :, 1], from_a1.at[s, 1], left)

    def add(target, *sources):
        value = target[...].astype(F32)
        for source in sources:
            value = value + source[...].astype(F32)
        target[...] = value.astype(BF16)

    def step_a2(s):
        receive(f"a1r{s}", from_a1.at[s, 0], left)
        add(part_a.at[at[1], s, :, 0], from_a1.at[s, 0])
        send(f"a2r{s}", part_a.at[at[1], s], from_a2.at[s, 0], right)
        receive(f"a1l{s}", from_a1.at[s, 1], right)
        add(part_a.at[at[3], s, :, 1], from_a1.at[s, 1])
        send(f"a2l{s}", part_a.at[at[3], s], from_a2.at[s, 1], left)

    def step_b2(s):
        receive(f"b1{s}2", from_b1.at[s, 2], across)
        add(part_b.at[at[2], s, y], from_b1.at[s, 2])
        send(f"b2r{s}", part_b.at[at[2], s, y, 0], from_b2.at[s, 0], right)
        send(f"b2l{s}", part_b.at[at[2], s, y, 1], from_b2.at[s, 1], left)

    def step_b3(s):
        receive(f"b1{s}1", from_b1.at[s, 1], across)
        receive(f"b2r{s}", from_b2.at[s, 0], left)
        add(part_b.at[at[1], s, y, 0], from_b1.at[s, 1, 0], from_b2.at[s, 0])
        add(part_b.at[at[1], s, y, 1], from_b1.at[s, 1, 1])
        send(f"b3r{s}", part_b.at[at[1], s, y], from_b3.at[s, 0], right)
        receive(f"b1{s}3", from_b1.at[s, 3], across)
        receive(f"b2l{s}", from_b2.at[s, 1], right)
        add(part_b.at[at[3], s, y, 0], from_b1.at[s, 3, 0])
        add(part_b.at[at[3], s, y, 1], from_b1.at[s, 3, 1], from_b2.at[s, 1])
        send(f"b3l{s}", part_b.at[at[3], s, y], from_b3.at[s, 1], left)

    def step_a3(s):
        receive(f"a2r{s}", from_a2.at[s, 0], left)
        receive(f"a2l{s}", from_a2.at[s, 1], right)
        add(part_a.at[at[0], s, mate], from_a2.at[s, 0, mate], from_a2.at[s, 1, mate])
        send(f"a3{s}", part_a.at[at[0], s, mate], from_a3.at[s], across)

    def update(s, which, sources):
        product = sources[0][...].astype(F32)
        for source in sources[1:]:
            product = product + source[...].astype(F32)
        product = product.reshape(half, kv)
        start = sub * s + half * which
        rows = slice(start, start + half)
        own = master[rows]
        column = gain_cols[rows]
        new = own - learn_rate * (product * jnp.concatenate([column, column], 1))
        upd[rows] = new
        payload[s, which, 0:half] = new.astype(BF16)
        share = own.astype(BF16).astype(F32) * product
        gain_gradient = jnp.sum((share[:, :128] + share[:, 128:]).T, 0, keepdims=True)
        new_gain = gains[:, rows] - gain_rate * gain_gradient
        upd_gain[:, rows] = new_gain
        payload[s, which, half : half + 16] = jnp.broadcast_to(
            jnp.concatenate([new_gain, new_gain], 1), (16, kv)
        ).astype(BF16)
        send(f"p{s}{which}", payload.at[s, which], other.at[s, which], ahead)

    def step_b4(s):
        receive(f"b1{s}0", from_b1.at[s, 0], across)
        receive(f"b3r{s}", from_b3.at[s, 0], left)
        receive(f"b3l{s}", from_b3.at[s, 1], right)
        update(s, 1, [part_b.at[at[0], s, y], from_b1.at[s, 0], from_b3.at[s, 0], from_b3.at[s, 1]])

    def step_a4(s):
        receive(f"a3{s}", from_a3.at[s], across)
        update(
            s, 0,
            [part_a.at[at[0], s, y], from_a2.at[s, 0, y], from_a2.at[s, 1, y], from_a3.at[s]],
        )

    def average(s, which):
        receive(f"p{s}{which}", other.at[s, which], behind)
        start = sub * s + half * which
        rows = slice(start, start + half)
        weight_out[0, rows] = 0.5 * (upd[rows] + other[s, which, 0:half].astype(F32))
        theirs_now = other[s, which, half : half + 16].astype(F32)[0:1, :half]
        gain_out[:, rows] = 0.5 * (upd_gain[:, rows] + theirs_now)

    def forward(j, q, first=False):
        value = jnp.dot(
            tok[at[j], rows_y[q]], whole_w[at[j], rows_y[q]].reshape(shard, kv),
            preferred_element_type=F32,
        )
        total[...] = value if first else total[...] + value

    def gather_2():
        receive("g1y", whole_w.at[x, mate], across)
        send("g2pr", whole_w.at[x, mate, 0], whole_w.at[x, mate, 0], right)
        send("g2pl", whole_w.at[x, mate, 0], whole_w.at[x, mate, 0], left)
        receive("g1r", whole_w.at[at[3], y], left)
        send("g2r", whole_w.at[at[3], y, :, 0], whole_w.at[at[3], y, :, 0], right)
        send("g2yl", whole_w.at[at[3], y, 1], whole_w.at[at[3], y, 1], across)
        receive("g1l", whole_w.at[at[1], y], right)
        send("g2l", whole_w.at[at[1], y, :, 1], whole_w.at[at[1], y, :, 1], left)
        send("g2yr", whole_w.at[at[1], y, 1], whole_w.at[at[1], y, 1], across)

    def gather_3():
        receive("g2r", whole_w.at[at[2], y, :, 0], left)
        receive("g2l", whole_w.at[at[2], y, :, 1], right)
        send("g3y", whole_w.at[at[2], y, 1], whole_w.at[at[2], y, 1], across)
        receive("g2pr", whole_w.at[at[3], mate, 0], left)
        send("g3r", whole_w.at[at[3], mate, 0, 0], whole_w.at[at[3], mate, 0, 0], right)
        receive("g2pl", whole_w.at[at[1], mate, 0], right)
        send("g3l", whole_w.at[at[1], mate, 0, 1], whole_w.at[at[1], mate, 0, 1], left)

    step_a2(0)
    step_b2(0)
    step_a2(1)
    step_b3(0)
    step_b2(1)
    step_a3(0)
    step_b4(0)
    step_b3(1)
    step_a3(1)
    gather_2()
    forward(0, 0, True)
    step_a4(0)
    step_b4(1)
    step_a4(1)
    forward(0, 1)
    forward(1, 0)
    gather_3()
    forward(3, 0)
    forward(2, 0)
    receive("g2yl", whole_w.at[at[3], mate, 1], across)
    forward(3, 1)
    receive("g2yr", whole_w.at[at[1], mate, 1], across)
    forward(1, 1)
    receive("g3r", whole_w.at[at[2], mate, 0, 0], left)
    receive("g3l", whole_w.at[at[2], mate, 0, 1], right)
    receive("g3y", whole_w.at[at[2], mate, 1], across)
    forward(2, 1)
    send("out", total.at[theirs], from_sibling, sibling)
    average(0, 1)
    average(0, 0)
    average(1, 1)
    average(1, 0)
    receive("out", from_sibling, sibling)
    factor = inverse[...]
    kv_out[...] = (
        (total[0:n_tok] + from_sibling[...]) * jnp.concatenate([factor, factor], 1)
    ).astype(BF16)
    for copy in sent:
        copy.wait_send()


def step_at(distance, collective, n_rep, tokens, cotangent, weight, gain):
    n_tok, width = tokens.shape
    _, shard, kv = weight.shape
    quarter = shard // N_SUB // 4
    half = 2 * quarter
    any_space = pl.BlockSpec(memory_space=pl.ANY)
    vmem = pl.BlockSpec(memory_space=pltpu.VMEM)
    return pl.pallas_call(
        functools.partial(kernel, distance, n_rep),
        out_shape=(
            jax.ShapeDtypeStruct((n_tok, kv), BF16),
            jax.ShapeDtypeStruct(weight.shape, F32),
            jax.ShapeDtypeStruct(gain.shape, F32),
        ),
        in_specs=[any_space] * 4,
        out_specs=(vmem, vmem, vmem),
        scratch_shapes=[
            pltpu.VMEM((4, 2, 2 * n_tok, shard), BF16),
            pltpu.VMEM((8, n_tok, shard), BF16),
            pltpu.VMEM((n_tok, kv), BF16),
            pltpu.VMEM((shard, kv), F32),
            pltpu.VMEM((1, shard), F32),
            pltpu.VMEM((shard, 128), F32),
            pltpu.VMEM((2 * n_tok, kv), BF16),
            pltpu.VMEM((n_tok, 128), F32),
            pltpu.VMEM((4, N_SUB, 2, 2, quarter, kv), BF16),
            pltpu.VMEM((4, N_SUB, 2, 2, quarter, kv), BF16),
            pltpu.VMEM((4, 2, 2, 2, shard // 4, kv), BF16),
            pltpu.VMEM((N_SUB, 2, 2, quarter, kv), BF16),
            pltpu.VMEM((N_SUB, 2, 2, 2, quarter, kv), BF16),
            pltpu.VMEM((N_SUB, 2, quarter, kv), BF16),
            pltpu.VMEM((N_SUB, 4, 2, quarter, kv), BF16),
            pltpu.VMEM((N_SUB, 2, quarter, kv), BF16),
            pltpu.VMEM((N_SUB, 2, 2, quarter, kv), BF16),
            pltpu.VMEM((N_SUB, 2, half + 16, kv), BF16),
            pltpu.VMEM((N_SUB, 2, half + 16, kv), BF16),
            pltpu.VMEM((shard, kv), F32),
            pltpu.VMEM((1, shard), F32),
            pltpu.VMEM((2 * n_tok, kv), F32),
            pltpu.VMEM((n_tok, kv), F32),
            pltpu.SemaphoreType.DMA((19,)),
            pltpu.SemaphoreType.DMA((MESSAGES,)),
            pltpu.SemaphoreType.DMA((MESSAGES,)),
        ],
        compiler_params=pltpu.CompilerParams(
            collective_id=collective, has_side_effects=True, vmem_limit_bytes=48 * 2**20
        ),
        name=f"step_{distance}",
    )(tokens, cotangent, weight, gain)


def body(tokens, cotangent, weight, gain, step):
    n_rep = lax.axis_size("rep")
    levels = n_rep.bit_length() - 1
    branches = [functools.partial(step_at, 1 << bit, bit, n_rep) for bit in range(levels)]
    return lax.switch(step % levels, branches, tokens, cotangent, weight, gain)


def solution(mesh):
    return jax.shard_map(
        body,
        mesh=mesh,
        in_specs=(
            P(("rep", "fsdp"), None),
            P(("rep", "fsdp"), None),
            P("rep", "fsdp", None),
            P("rep", "fsdp"),
            P(),
        ),
        out_specs=(P(("rep", "fsdp"), None), P("rep", "fsdp", None), P("rep", "fsdp")),
        check_vma=False,
    )
```

time: 166 us -> 71.7 us (0.43)
  the two profiles are of different devices: /device:TPU:1 before, /device:TPU:32 now
where the time goes in v1:
time: 71.7 us; the launch traced here: 71.5 us
  Pallas kernels  62.3 us (87%)
  loops' own time  5.87 us (8%)
  local copies, waits for them, and re-layouts  2.02 us (3%)
  between operations  1.3 us (2%)
    pallas_call x1, Pallas kernels, step_at(): pl.pallas_call(functools.partial(kernel, distance, n_rep), out_shape=(jax...  62.3 us
    another operation x1, loops' own time, body(): return lax.switch(step % levels, branches, tokens, cotangent, weight, gain)  5.87 us
    unnamed x3, local copies, waits for them, and re-layouts  2.02 us

profile of v1, /device:TPU:32, one launch (start us, length us, event | category | flops | bytes accessed | tf_op | source)
XLA Modules:
  0.0 71.5 jit_solution(11798433110410689225)
XLA Ops:
  1.3 68.2 %conditional.1 = ((bf16[224,256]{1,0:T(8,128)(2,1)S(1)}, f32[1,512,256]{2,1,0:T(8,128)S(1)}, f32[1,512]{1,0:T(1,128)S(1)})) conditional(s32[]{:T(128)} %clamp.3, (bf16[224,8192]{1,0:T(8,128)(2,1)}, bf16[224,256]{1,0:T(8,128)(2,1)}, f32[1,512,256]{2,1,0:T(8,128)}, f32[1,512]{1,0:T(1,128)}) %tuple.22, ...), branch_computations={%region_0.1_spmd, %region_1.2_spmd, %region_2.3_spmd, %region_3.4_... | conditional | bytes 8 | solution.py:339
  6.9 62.3 %step_16.1 = (bf16[224,256]{1,0:T(8,128)(2,1)S(1)}, f32[1,512,256]{2,1,0:T(8,128)S(1)}, f32[1,512]{1,0:T(1,128)S(1)}) custom-call(bf16[224,8192]{1,0:T(8,128)(2,1)} %get-tuple-element.56.tokens, bf16[224,256]{1,0:T(8,128)(2,1)} %get-tuple-element.57.cotangent, f32[1,512,256]{2,1,0:T(8,128)} %get-tuple-element.58.weight, f32[1,512]{1,0:T(1,128)} %get-tuple-element.59.gain), custom_call_target="tpu_custom_call" | custom-call | tf_op jit(solution)/shard_map/cond/branch_4_fun/step_16/pallas_call | solution.py:291
  69.5 0.6 copy.42
  70.2 0.8 %copy.43 = f32[1,512,256]{2,1,0:T(8,128)} copy(f32[1,512,256]{2,1,0:T(8,128)S(1)} %get-tuple-element.100) | data formatting | bytes 1048576
  71.0 0.6 copy.44
